TPU v7x, 32 devices: a whole 2x2x4 slice. The times are simulated.
32 devices in a mesh: groups: 2 (over y), row: 2 (over x), col: 4 (over z), head: 2 (over core).
Axes of the slice: x: 2, y: 2, z: 4, core: 2. Of those that a mesh axis runs over, the one named last changes fastest.
Arguments:
- pair_rep: bfloat16 [96, 48, 128], P(('groups', 'col'), 'row'), parts along dimension 0, may hold values from -4.5 to 4.5
- pad_mask: int32 [96], P('groups'), parts along dimension 0, may hold values from 0 to 1, as said below
- chain_breaks: int32 [8], P('groups'), parts along dimension 0, may hold values from 1 to 47, as said below
- w_query: bfloat16 [128, 128], P(None, 'head'), may hold values from -0.5 to 0.5
- w_key: bfloat16 [128, 128], P(None, 'head'), may hold values from -0.5 to 0.5
- w_value: bfloat16 [128, 128], P(None, 'head'), may hold values from -0.5 to 0.5
- w_gate: bfloat16 [128, 128], P(None, 'head'), may hold values from -0.5 to 0.5
- w_bias: bfloat16 [128, 4], P(None, 'head'), may hold values from -8 to 8
- chain_bias: float32 [4], P('head'), may hold values from -2 to 2
- w_out: bfloat16 [128, 128], P('head'), may hold values from -6 to 6
Outputs:
- update: bfloat16 [96, 48, 128], P(('groups', 'col'), 'row', 'head'), parts along dimension 0
There are 2 independent parts, one for each index of `groups`. A program takes and returns all parts, laid end to end along the dimension named above; an argument that names none is the same for every part. Nothing has to cross between parts.
Inputs may be any that keep to these rules, and one draw needn't show every extreme that they name: `pad_mask`: 1 on a prefix of 24 to 42 residues and 0 after it. `chain_breaks`: strictly increasing.
All inputs are finite; a program needn't handle non-finite values.
Results may differ from a plain program's by a relative error of at most 0.014.
Values may be sent and summed in bfloat16 or wider, within the bound.
A program may use at most 64 MiB of HBM per device.

v0:
```python
import functools

import jax
import jax.numpy as jnp
from jax import lax
from jax.experimental import pallas as pl
from jax.experimental.pallas import tpu as pltpu
from jax.sharding import PartitionSpec as P

HD = 32
MESH = pl.DeviceIdType.MESH
F32 = jnp.float32
BF16 = jnp.bfloat16
NT = (((1,), (1,)), ((), ()))


def layer_norm(x):
    centred = x - jnp.mean(x, axis=-1, keepdims=True)
    spread = jnp.mean(centred * centred, axis=-1, keepdims=True)
    return centred * lax.rsqrt(spread + 1e-05)


def dot(a, b):
    return jnp.dot(a, b, preferred_element_type=F32)


def dot_t(a, b):
    return lax.dot_general(a, b, NT, preferred_element_type=F32)


def largest_divisor(n, limit, step=1):
    best = step
    for d in range(step, n + 1, step):
        if n % d == 0 and d <= limit:
            best = d
    return best


def kernel(
    sizes,
    pair, mask, breaks, chain_bias, wq, wk, wv, wg, wb, wo,
    out,
    xs, wbuf, wbbuf, wobuf, maskbuf, breakbuf, cbbuf, qg, kv, bsend, brecv, bfull, gown, goth,
    local_sem, x_send, x_recv, wo_send, wo_recv, b_send, b_recv, g_send, g_recv,
):
    rows, cols, heads, n_i, n_j, n_h, channels = sizes
    n_k = rows * n_j
    hw = n_h * HD
    piece = bsend.shape[2]
    r, c, h = lax.axis_index("row"), lax.axis_index("col"), lax.axis_index("head")

    barrier = pltpu.get_barrier_semaphore()
    for r2 in range(rows):
        for c2 in range(cols):
            @pl.when(jnp.logical_or(r != r2, c != c2))
            def _():
                pl.semaphore_signal(
                    barrier, inc=1, device_id={"row": r2, "col": c2}, device_id_type=MESH
                )
    for d in range(1, heads):
        pl.semaphore_signal(
            barrier, inc=1, device_id={"head": lax.rem(h + d, heads)}, device_id_type=MESH
        )

    locals_ = [
        pltpu.make_async_copy(pair, xs.at[r], local_sem.at[0]),
        pltpu.make_async_copy(wb, wbbuf, local_sem.at[1]),
        pltpu.make_async_copy(wq, wbuf.at[0, pl.ds(0, hw)], local_sem.at[2]),
        pltpu.make_async_copy(wg, wbuf.at[0, pl.ds(hw, hw)], local_sem.at[3]),
        pltpu.make_async_copy(wk, wbuf.at[1, pl.ds(0, hw)], local_sem.at[4]),
        pltpu.make_async_copy(wv, wbuf.at[1, pl.ds(hw, hw)], local_sem.at[5]),
        pltpu.make_async_copy(wo, wobuf.at[0], local_sem.at[6]),
        pltpu.make_async_copy(mask, maskbuf, local_sem.at[7]),
        pltpu.make_async_copy(breaks, breakbuf, local_sem.at[8]),
        pltpu.make_async_copy(chain_bias, cbbuf, local_sem.at[9]),
    ]
    for copy in locals_:
        copy.start()

    pl.semaphore_wait(barrier, rows * cols - 1 + heads - 1)

    x_copies = []
    for d in range(1, rows):
        copy = pltpu.make_async_remote_copy(
            src_ref=pair, dst_ref=xs.at[r], send_sem=x_send.at[d], recv_sem=x_recv.at[d],
            device_id={"row": lax.rem(r + d, rows)}, device_id_type=MESH,
        )
        copy.start()
        x_copies.append(copy)
    wo_copies = []
    for d in range(1, heads):
        copy = pltpu.make_async_remote_copy(
            src_ref=wo, dst_ref=wobuf.at[d], send_sem=wo_send.at[d], recv_sem=wo_recv.at[d],
            device_id={"head": lax.rem(h + d, heads)}, device_id_type=MESH,
        )
        copy.start()
        wo_copies.append(copy)

    for copy in locals_:
        copy.wait()

    wqg, wkv = wbuf[0], wbuf[1]
    wbt = jnp.concatenate(
        [wbbuf[...].astype(F32), jnp.zeros((16 - n_h, channels), F32)], axis=0
    ).astype(BF16)

    lane = lax.broadcasted_iota(jnp.int32, (1, 2 * hw), 1)
    step_i = largest_divisor(n_i, 12, 2)
    flat = step_i * n_j
    own_normed = []
    for first in range(0, n_i, step_i):
        normed = layer_norm(xs[r, pl.ds(first * n_j, flat), :].astype(F32))
        normed3 = normed.reshape(step_i, n_j, channels).astype(BF16)
        for i in range(step_i):
            line = lax.dot_general(wbt, normed3[i], NT, preferred_element_type=F32)
            p, at = divmod(first + i, piece)
            for head in range(n_h):
                bsend[p, head, pl.ds(at, 1), :] = line[head : head + 1]
        own_normed.append(normed.astype(BF16))

    def bias_copy(p, c2):
        start = c * n_i + p * piece
        target = start // n_j
        slot = (start - target * n_j) // piece
        return target, slot, pltpu.make_async_remote_copy(
            src_ref=bsend.at[p], dst_ref=brecv.at[r, slot],
            send_sem=b_send.at[p, c2], recv_sem=b_recv.at[r, slot],
            device_id={"row": target, "col": c2}, device_id_type=MESH,
        )

    pieces_sent = n_i // piece
    for p in range(pieces_sent):
        for c2 in range(cols):
            target, slot, copy = bias_copy(p, c2)
            here = jnp.logical_and(target == r, c == c2)

            @pl.when(jnp.logical_not(here))
            def _():
                copy.start()

            @pl.when(here)
            def _():
                brecv[r, slot] = bsend[p]

    for step, first in enumerate(range(0, n_i, step_i)):
        at = pl.ds(first * n_j, flat)
        both = dot_t(own_normed[step], wqg)
        qg[at, :] = jnp.where(
            lane < hw, (both * HD ** (-0.5)).astype(BF16).astype(F32),
            jax.nn.sigmoid(both).astype(BF16).astype(F32),
        )
        kv[r, at, :] = dot_t(own_normed[step], wkv)

    key_pos = lax.broadcasted_iota(jnp.int32, (n_j, n_k), 1)
    query_pos = r * n_j + lax.broadcasted_iota(jnp.int32, (n_j, n_k), 0)
    key_chain = jnp.zeros((n_j, n_k), jnp.int32)
    query_chain = jnp.zeros((n_j, n_k), jnp.int32)
    for b in range(breaks.shape[0]):
        key_chain += (breakbuf[b] <= key_pos).astype(jnp.int32)
        query_chain += (breakbuf[b] <= query_pos).astype(jnp.int32)
    across = (key_chain != query_chain).astype(F32)
    mask_term = (maskbuf[...].astype(F32) - 1.0) * 1000000000.0

    own_rows = wobuf.shape[1]
    share = wobuf.shape[2] // heads

    def out_weight(d):
        full = wobuf[d].astype(F32)
        mine = full[:, :share]
        for t in range(1, heads):
            mine = jnp.where(h == t, full[:, t * share : (t + 1) * share], mine)
        return jnp.concatenate([jnp.zeros((hw, share), F32), mine], axis=0).astype(BF16)

    for copy in wo_copies:
        copy.wait()
    out_weights = [out_weight(d) for d in range(heads)]

    for d in range(1, rows):
        x_copies[d - 1].wait()
        source = lax.rem(r + rows - d, rows)
        for first in range(0, n_i, step_i):
            at = pl.ds(first * n_j, flat)
            normed = layer_norm(xs[source, at, :].astype(F32)).astype(BF16)
            kv[source, at, :] = dot_t(normed, wkv)

    slots = n_j // piece
    for slot in range(slots):
        source_c = (r * n_j + slot * piece) // n_i
        for r2 in range(rows):
            @pl.when(jnp.logical_or(r2 != r, source_c != c))
            def _():
                pltpu.make_async_remote_copy(
                    src_ref=bsend.at[0], dst_ref=brecv.at[r2, slot],
                    send_sem=b_send.at[0, 0], recv_sem=b_recv.at[r2, slot],
                    device_id={"row": r2}, device_id_type=MESH,
                ).wait_recv()
    for slot in range(slots):
        for r2 in range(rows):
            for head in range(n_h):
                bfull[head, pl.ds(slot * piece, piece), pl.ds(r2 * n_j, n_j)] = brecv[
                    r2, slot, head
                ]
    bias = jnp.concatenate(
        [bfull[head] + (cbbuf[head] * across + mask_term) for head in range(n_h)], axis=0
    )

    lanes_k = -(-n_k // 128) * 128
    step_a = largest_divisor(n_i, max(2, 40 * 1024 // (n_h * n_j * lanes_k)), 2)
    flat_a = step_a * n_j
    steps = n_i // step_a

    def gated_copy(step, d, at):
        return pltpu.make_async_remote_copy(
            src_ref=gown.at[at, :], dst_ref=goth.at[d, at, :],
            send_sem=g_send.at[d, step], recv_sem=g_recv.at[d, step],
            device_id={"head": lax.rem(h + d, heads)}, device_id_type=MESH,
        )

    def attend(step):
        at = pl.ds(pl.multiple_of(step * flat_a, 16), flat_a)
        qg3 = qg[at, :].reshape(step_a, n_j, 2 * hw)
        queries = jnp.concatenate(
            [
                jnp.where(jnp.logical_and(lane >= t * HD, lane < (t + 1) * HD)[None], qg3, 0.0)
                for t in range(n_h)
            ],
            axis=1,
        ).astype(BF16)
        keys = jnp.concatenate(
            [kv[r2, at, :].reshape(step_a, n_j, 2 * hw) for r2 in range(rows)], axis=1
        ).astype(BF16)
        scores = lax.dot_general(
            queries, keys, (((2,), (2,)), ((0,), (0,))), preferred_element_type=F32
        ) + bias[None]
        weights = jnp.exp(scores - jnp.max(scores, axis=-1, keepdims=True))
        total = jnp.sum(weights, axis=-1, keepdims=True)
        mixed = lax.dot_general(
            weights.astype(BF16), keys, (((2,), (1,)), ((0,), (0,))), preferred_element_type=F32
        ) / total
        attended = mixed[:, :n_j]
        for t in range(1, n_h):
            attended = jnp.where(
                (lane >= hw + t * HD)[None], mixed[:, t * n_j : (t + 1) * n_j], attended
            )
        gated = jnp.where(
            (lane >= hw)[None], attended.astype(BF16).astype(F32) * qg3, 0.0
        )
        gown[at, :] = gated.reshape(flat_a, 2 * hw).astype(BF16)
        for d in range(1, heads):
            gated_copy(step, d, at).start()

    def project(step):
        at = pl.ds(pl.multiple_of(step * flat_a, 16), flat_a)
        acc = dot(gown[at, :], out_weights[0])
        for d in range(1, heads):
            gated_copy(step, d, at).wait()
            acc += dot(goth[d, at, :], out_weights[d])
        out[at, :] = acc.astype(out.dtype)

    if steps <= 4:
        for step in range(steps):
            attend(step)
        for step in range(steps):
            project(step)
    else:
        pl.loop(0, steps)(attend)
        pl.loop(0, steps)(project)

    for p in range(pieces_sent):
        for c2 in range(cols):
            target, slot, copy = bias_copy(p, c2)

            @pl.when(jnp.logical_or(target != r, c != c2))
            def _():
                copy.wait_send()


def per_device(
    mesh_sizes, pair_rep, pad_mask, chain_breaks, w_query, w_key, w_value, w_gate, w_bias,
    chain_bias, w_out
):
    rows, cols, heads = mesh_sizes
    n_i, n_j, channels = pair_rep.shape
    n_h = chain_bias.shape[0]
    hw = n_h * HD
    n_k = rows * n_j
    total = n_i * n_j
    piece = min(n_i, n_j)
    lanes_k = -(-n_k // 128) * 128
    step_a = largest_divisor(n_i, max(2, 40 * 1024 // (n_h * n_j * lanes_k)), 2)
    steps = n_i // step_a
    share = w_out.shape[1] // heads
    hbm = pl.BlockSpec(memory_space=pltpu.HBM)
    vmem = pl.BlockSpec(memory_space=pltpu.VMEM)
    dma = pltpu.SemaphoreType.DMA
    scratch = [
        pltpu.VMEM((rows, total, channels), BF16),
        pltpu.VMEM((2, 2 * hw, channels), BF16),
        pltpu.VMEM((n_h, channels), BF16),
        pltpu.VMEM((heads, hw, w_out.shape[1]), BF16),
        pltpu.VMEM((1, n_k), jnp.int32),
        pltpu.SMEM(chain_breaks.shape, jnp.int32),
        pltpu.SMEM(chain_bias.shape, F32),
        pltpu.VMEM((total, 2 * hw), F32),
        pltpu.VMEM((rows, total, 2 * hw), F32),
        pltpu.VMEM((n_i // piece, n_h, piece, n_j), F32),
        pltpu.VMEM((rows, n_j // piece, n_h, piece, n_j), F32),
        pltpu.VMEM((n_h, n_j, n_k), F32),
        pltpu.VMEM((total, 2 * hw), BF16),
        pltpu.VMEM((heads, total, 2 * hw), BF16),
        dma((10,)),
        dma((rows,)),
        dma((rows,)),
        dma((heads,)),
        dma((heads,)),
        dma((n_i // piece, cols)),
        dma((rows, n_j // piece)),
        dma((heads, steps)),
        dma((heads, steps)),
    ]
    update = pl.pallas_call(
        functools.partial(kernel, (rows, cols, heads, n_i, n_j, n_h, channels)),
        out_shape=jax.ShapeDtypeStruct((total, share), BF16),
        in_specs=[hbm] * 10,
        out_specs=vmem,
        scratch_shapes=scratch,
        compiler_params=pltpu.CompilerParams(
            collective_id=0,
            has_side_effects=True,
            vmem_limit_bytes=60 << 20,
        ),
    )(
        pair_rep.reshape(total, channels), pad_mask.reshape(1, n_k), chain_breaks, chain_bias,
        w_query.T, w_key.T, w_value.T, w_gate.T, w_bias.T, w_out,
    )
    return update.reshape(n_i, n_j, share)


def solution(mesh):
    placed = (
        P(("groups", "col"), "row", None),
        P("groups"),
        P("groups"),
        P(None, "head"),
        P(None, "head"),
        P(None, "head"),
        P(None, "head"),
        P(None, "head"),
        P("head"),
        P("head", None),
    )
    sizes = (mesh.shape["row"], mesh.shape["col"], mesh.shape["head"])
    return jax.shard_map(
        functools.partial(per_device, sizes),
        mesh=mesh,
        in_specs=placed,
        out_specs=P(("groups", "col"), "row", "head"),
        check_vma=False,
    )
```

profile of v0, /device:TPU:0, one launch (start us, length us, event | category | flops | bytes accessed | tf_op | source)
XLA Modules:
  0.0 13.9 jit_solution(9702989989280175749)
XLA Ops:
  0.0 12.3 %shard_map.100 = bf16[288,64]{1,0:T(8,128)(2,1)} custom-call(bf16[288,128]{1,0:T(8,128)(2,1)} %bitcast.9, s32[1,48]{1,0:T(1,128)} %bitcast.14, s32[4]{0:T(128)} %breaks.1, f32[2]{0:T(128)} %chain_bias.1, bf16[64,128]{1,0:T(8,128)(2,1)} %bitcast.10, bf16[64,128]{1,0:T(8,128)(2,1)} %bitcast.11, bf16[64,128]{1,0:T(8,128)(2,1)} %bitcast.12, ...), custom_call_target="tpu_custom_call" | custom-call | tf_op jit(solution)/shard_map/pallas_call | solution.py:321
  12.3 1.5 %copy.12 = bf16[12,24,64]{2,1,0:T(8,128)(2,1)} copy(bf16[12,24,64]{2,1,0:T(8,128)(2,1)} %bitcast.8) | data formatting | bytes 73728
where the time goes:
time: 14 us; the launch traced here: 13.9 us
  Pallas kernels  12.3 us (88%)
  local copies, waits for them, and re-layouts  1.52 us (11%)
    pallas_call x1, Pallas kernels, per_device(): pl.pallas_call(functools.partial(kernel, (rows, cols, heads, n_i, n_j, n_...  12.3 us
    unnamed x1, local copies, waits for them, and re-layouts  1.52 us

commit v1 on v0

--- a/solution.py
+++ b/solution.py
@@ -39,9 +39,9 @@
 def kernel(
     sizes,
     pair, mask, breaks, chain_bias, wq, wk, wv, wg, wb, wo,
-    out,
-    xs, wbuf, wbbuf, wobuf, maskbuf, breakbuf, cbbuf, qg, kv, bsend, brecv, bfull, gown, goth,
-    local_sem, x_send, x_recv, wo_send, wo_recv, b_send, b_recv, g_send, g_recv,
+    gout, owout,
+    xs, wbuf, wbbuf, wobuf, maskbuf, breakbuf, cbbuf, qg, kv, bsend, brecv, bfull, gown, owbuf,
+    local_sem, x_send, x_recv, wo_send, wo_recv, b_send, b_recv, g_send, g_recv, own_sem,
 ):
     rows, cols, heads, n_i, n_j, n_h, channels = sizes
     n_k = rows * n_j
@@ -173,7 +173,10 @@
 
     for copy in wo_copies:
         copy.wait()
-    out_weights = [out_weight(d) for d in range(heads)]
+    for d in range(heads):
+        owbuf[d] = out_weight(d)
+    weight_out = pltpu.make_async_copy(owbuf, owout, local_sem.at[10])
+    weight_out.start()
 
     for d in range(1, rows):
         x_copies[d - 1].wait()
@@ -211,10 +214,13 @@
 
     def gated_copy(step, d, at):
         return pltpu.make_async_remote_copy(
-            src_ref=gown.at[at, :], dst_ref=goth.at[d, at, :],
+            src_ref=gown.at[at, :], dst_ref=gout.at[d, at, :],
             send_sem=g_send.at[d, step], recv_sem=g_recv.at[d, step],
             device_id={"head": lax.rem(h + d, heads)}, device_id_type=MESH,
         )
+
+    def own_copy(step, at):
+        return pltpu.make_async_copy(gown.at[at, :], gout.at[0, at, :], own_sem.at[step])
 
     def attend(step):
         at = pl.ds(pl.multiple_of(step * flat_a, 16), flat_a)
@@ -248,23 +254,23 @@
         gown[at, :] = gated.reshape(flat_a, 2 * hw).astype(BF16)
         for d in range(1, heads):
             gated_copy(step, d, at).start()
-
-    def project(step):
+        own_copy(step, at).start()
+
+    def finish(step):
         at = pl.ds(pl.multiple_of(step * flat_a, 16), flat_a)
-        acc = dot(gown[at, :], out_weights[0])
+        own_copy(step, at).wait()
         for d in range(1, heads):
             gated_copy(step, d, at).wait()
-            acc += dot(goth[d, at, :], out_weights[d])
-        out[at, :] = acc.astype(out.dtype)
 
     if steps <= 4:
         for step in range(steps):
             attend(step)
         for step in range(steps):
-            project(step)
+            finish(step)
     else:
         pl.loop(0, steps)(attend)
-        pl.loop(0, steps)(project)
+        pl.loop(0, steps)(finish)
+    weight_out.wait()
 
     for p in range(pieces_sent):
         for c2 in range(cols):
@@ -273,6 +279,13 @@
             @pl.when(jnp.logical_or(target != r, c != c2))
             def _():
                 copy.wait_send()
+
+
+def project(gated, weights, out):
+    acc = dot(gated[0], weights[0])
+    for d in range(1, gated.shape[0]):
+        acc += dot(gated[d], weights[d])
+    out[...] = acc.astype(out.dtype)
 
 
 def per_device(
@@ -307,8 +320,8 @@
         pltpu.VMEM((rows, n_j // piece, n_h, piece, n_j), F32),
         pltpu.VMEM((n_h, n_j, n_k), F32),
         pltpu.VMEM((total, 2 * hw), BF16),
-        pltpu.VMEM((heads, total, 2 * hw), BF16),
-        dma((10,)),
+        pltpu.VMEM((heads, 2 * hw, share), BF16),
+        dma((11,)),
         dma((rows,)),
         dma((rows,)),
         dma((heads,)),
@@ -317,12 +330,16 @@
         dma((rows, n_j // piece)),
         dma((heads, steps)),
         dma((heads, steps)),
+        dma((steps,)),
     ]
-    update = pl.pallas_call(
+    gated, weights = pl.pallas_call(
         functools.partial(kernel, (rows, cols, heads, n_i, n_j, n_h, channels)),
-        out_shape=jax.ShapeDtypeStruct((total, share), BF16),
+        out_shape=[
+            jax.ShapeDtypeStruct((heads, total, 2 * hw), BF16),
+            jax.ShapeDtypeStruct((heads, 2 * hw, share), BF16),
+        ],
         in_specs=[hbm] * 10,
-        out_specs=vmem,
+        out_specs=[hbm, hbm],
         scratch_shapes=scratch,
         compiler_params=pltpu.CompilerParams(
             collective_id=0,
@@ -333,6 +350,13 @@
         pair_rep.reshape(total, channels), pad_mask.reshape(1, n_k), chain_breaks, chain_bias,
         w_query.T, w_key.T, w_value.T, w_gate.T, w_bias.T, w_out,
     )
+    update = pl.pallas_call(
+        project,
+        out_shape=jax.ShapeDtypeStruct((total, share), BF16),
+        in_specs=[vmem, vmem],
+        out_specs=vmem,
+        compiler_params=pltpu.CompilerParams(vmem_limit_bytes=60 << 20),
+    )(gated, weights)
     return update.reshape(n_i, n_j, share)
 
 

time: 14 us -> 13.5 us (0.964)
  local copies, waits for them, and re-layouts: 1.52 us -> 0 us
  Pallas kernels: 12.3 us -> 13.4 us
    pallas_call x0 -> x1, Pallas kernels: none -> 1.72 us  [per_device(): pl.pallas_call(project, out_shape=jax.ShapeDtypeStruct((total, share), BF...]
    unnamed x1 -> x0, local copies, waits for them, and re-layouts: 1.52 us -> none
    pallas_call x1, Pallas kernels: 12.3 us -> 11.7 us  [per_device(): pl.pallas_call(functools.partial(kernel, (rows, cols, heads, n_i, n_j, n_...]
where the time goes in v1:
time: 13.5 us; the launch traced here: 13.4 us
  Pallas kernels  13.4 us (99%)
    pallas_call x1, Pallas kernels, per_device(): pl.pallas_call(functools.partial(kernel, (rows, cols, heads, n_i, n_j, n_...  11.7 us
    pallas_call x1, Pallas kernels, per_device(): pl.pallas_call(project, out_shape=jax.ShapeDtypeStruct((total, share), BF...  1.72 us

profile of v1, /device:TPU:0, one launch (start us, length us, event | category | flops | bytes accessed | tf_op | source)
XLA Modules:
  0.0 13.4 jit_solution(11176975295715041172)
XLA Ops:
  0.0 11.7 %shard_map.100 = (bf16[2,288,128]{2,1,0:T(8,128)(2,1)}, bf16[2,128,64]{2,1,0:T(8,128)(2,1)}) custom-call(bf16[288,128]{1,0:T(8,128)(2,1)} %bitcast.8, s32[1,48]{1,0:T(1,128)} %bitcast.13, s32[4]{0:T(128)} %breaks.1, f32[2]{0:T(128)} %chain_bias.1, bf16[64,128]{1,0:T(8,128)(2,1)} %bitcast.9, bf16[64,128]{1,0:T(8,128)(2,1)} %bitcast.10, ...), custom_call_target="tpu_custom_call" | custom-call | tf_op jit(solution)/shard_map/pallas_call | solution.py:335
  11.7 1.7 %shard_map.101 = bf16[288,64]{1,0:T(8,128)(2,1)} custom-call(bf16[2,288,128]{2,1,0:T(8,128)(2,1)} %get-tuple-element.7.gated, bf16[2,128,64]{2,1,0:T(8,128)(2,1)} %get-tuple-element.8.weights), custom_call_target="tpu_custom_call" | custom-call | tf_op jit(solution)/shard_map/pallas_call | solution.py:353

commit v2 on v1

--- a/solution.py
+++ b/solution.py
@@ -50,12 +50,17 @@
     r, c, h = lax.axis_index("row"), lax.axis_index("col"), lax.axis_index("head")
 
     barrier = pltpu.get_barrier_semaphore()
-    for r2 in range(rows):
-        for c2 in range(cols):
-            @pl.when(jnp.logical_or(r != r2, c != c2))
+    for d in range(1, rows):
+        pl.semaphore_signal(
+            barrier, inc=1, device_id={"row": lax.rem(r + d, rows)}, device_id_type=MESH
+        )
+    for slot in range(n_j // piece):
+        source_c = (r * n_j + slot * piece) // n_i
+        for r2 in range(rows):
+            @pl.when(jnp.logical_or(r2 != r, source_c != c))
             def _():
                 pl.semaphore_signal(
-                    barrier, inc=1, device_id={"row": r2, "col": c2}, device_id_type=MESH
+                    barrier, inc=1, device_id={"row": r2, "col": source_c}, device_id_type=MESH
                 )
     for d in range(1, heads):
         pl.semaphore_signal(
@@ -77,7 +82,11 @@
     for copy in locals_:
         copy.start()
 
-    pl.semaphore_wait(barrier, rows * cols - 1 + heads - 1)
+    copies_out = rows - 1 + heads - 1
+    for p in range(n_i // piece):
+        here = ((c * n_i + p * piece) // n_j == r).astype(jnp.int32)
+        copies_out = copies_out + cols - here
+    pl.semaphore_wait(barrier, copies_out)
 
     x_copies = []
     for d in range(1, rows):

time: 13.5 us -> 13.5 us (level)
  no operation moved by 1% of the time
where the time goes in v2:
time: 13.5 us; the launch traced here: 13.4 us
  Pallas kernels  13.4 us (99%)
    pallas_call x1, Pallas kernels, per_device(): pl.pallas_call(functools.partial(kernel, (rows, cols, heads, n_i, n_j, n_...  11.7 us
    pallas_call x1, Pallas kernels, per_device(): pl.pallas_call(project, out_shape=jax.ShapeDtypeStruct((total, share), BF...  1.73 us

profile of v2, /device:TPU:0, one launch (start us, length us, event | category | flops | bytes accessed | tf_op | source)
XLA Modules:
  0.0 13.4 jit_solution(12482198010551560532)
XLA Ops:
  0.0 11.7 %shard_map.100 = (bf16[2,288,128]{2,1,0:T(8,128)(2,1)}, bf16[2,128,64]{2,1,0:T(8,128)(2,1)}) custom-call(bf16[288,128]{1,0:T(8,128)(2,1)} %bitcast.8, s32[1,48]{1,0:T(1,128)} %bitcast.13, s32[4]{0:T(128)} %breaks.1, f32[2]{0:T(128)} %chain_bias.1, bf16[64,128]{1,0:T(8,128)(2,1)} %bitcast.9, bf16[64,128]{1,0:T(8,128)(2,1)} %bitcast.10, ...), custom_call_target="tpu_custom_call" | custom-call | tf_op jit(solution)/shard_map/pallas_call | solution.py:344
  11.7 1.7 %shard_map.101 = bf16[288,64]{1,0:T(8,128)(2,1)} custom-call(bf16[2,288,128]{2,1,0:T(8,128)(2,1)} %get-tuple-element.7.gated, bf16[2,128,64]{2,1,0:T(8,128)(2,1)} %get-tuple-element.8.weights), custom_call_target="tpu_custom_call" | custom-call | tf_op jit(solution)/shard_map/pallas_call | solution.py:362

commit v3 on v2

--- a/solution.py
+++ b/solution.py
@@ -82,29 +82,6 @@
     for copy in locals_:
         copy.start()
 
-    copies_out = rows - 1 + heads - 1
-    for p in range(n_i // piece):
-        here = ((c * n_i + p * piece) // n_j == r).astype(jnp.int32)
-        copies_out = copies_out + cols - here
-    pl.semaphore_wait(barrier, copies_out)
-
-    x_copies = []
-    for d in range(1, rows):
-        copy = pltpu.make_async_remote_copy(
-            src_ref=pair, dst_ref=xs.at[r], send_sem=x_send.at[d], recv_sem=x_recv.at[d],
-            device_id={"row": lax.rem(r + d, rows)}, device_id_type=MESH,
-        )
-        copy.start()
-        x_copies.append(copy)
-    wo_copies = []
-    for d in range(1, heads):
-        copy = pltpu.make_async_remote_copy(
-            src_ref=wo, dst_ref=wobuf.at[d], send_sem=wo_send.at[d], recv_sem=wo_recv.at[d],
-            device_id={"head": lax.rem(h + d, heads)}, device_id_type=MESH,
-        )
-        copy.start()
-        wo_copies.append(copy)
-
     for copy in locals_:
         copy.wait()
 
@@ -127,30 +104,6 @@
                 bsend[p, head, pl.ds(at, 1), :] = line[head : head + 1]
         own_normed.append(normed.astype(BF16))
 
-    def bias_copy(p, c2):
-        start = c * n_i + p * piece
-        target = start // n_j
-        slot = (start - target * n_j) // piece
-        return target, slot, pltpu.make_async_remote_copy(
-            src_ref=bsend.at[p], dst_ref=brecv.at[r, slot],
-            send_sem=b_send.at[p, c2], recv_sem=b_recv.at[r, slot],
-            device_id={"row": target, "col": c2}, device_id_type=MESH,
-        )
-
-    pieces_sent = n_i // piece
-    for p in range(pieces_sent):
-        for c2 in range(cols):
-            target, slot, copy = bias_copy(p, c2)
-            here = jnp.logical_and(target == r, c == c2)
-
-            @pl.when(jnp.logical_not(here))
-            def _():
-                copy.start()
-
-            @pl.when(here)
-            def _():
-                brecv[r, slot] = bsend[p]
-
     for step, first in enumerate(range(0, n_i, step_i)):
         at = pl.ds(first * n_j, flat)
         both = dot_t(own_normed[step], wqg)
@@ -170,6 +123,61 @@
     across = (key_chain != query_chain).astype(F32)
     mask_term = (maskbuf[...].astype(F32) - 1.0) * 1000000000.0
 
+    copies_out = rows - 1 + heads - 1
+    for p in range(n_i // piece):
+        here = ((c * n_i + p * piece) // n_j == r).astype(jnp.int32)
+        copies_out = copies_out + cols - here
+    pl.semaphore_wait(barrier, copies_out)
+
+    x_parts = 2 if n_i % 2 == 0 and (n_i // 2 * n_j) % 16 == 0 else 1
+    part_i = n_i // x_parts
+
+    def x_copy(d, part):
+        at = pl.ds(part * part_i * n_j, part_i * n_j)
+        return pltpu.make_async_remote_copy(
+            src_ref=pair.at[at, :], dst_ref=xs.at[r, at, :],
+            send_sem=x_send.at[d, part], recv_sem=x_recv.at[d, part],
+            device_id={"row": lax.rem(r + d, rows)}, device_id_type=MESH,
+        )
+
+    for d in range(1, rows):
+        x_copy(d, 0).start()
+    def bias_copy(p, c2):
+        start = c * n_i + p * piece
+        target = start // n_j
+        slot = (start - target * n_j) // piece
+        return target, slot, pltpu.make_async_remote_copy(
+            src_ref=bsend.at[p], dst_ref=brecv.at[r, slot],
+            send_sem=b_send.at[p, c2], recv_sem=b_recv.at[r, slot],
+            device_id={"row": target, "col": c2}, device_id_type=MESH,
+        )
+
+    pieces_sent = n_i // piece
+    for p in range(pieces_sent):
+        for c2 in range(cols):
+            target, slot, copy = bias_copy(p, c2)
+            here = jnp.logical_and(target == r, c == c2)
+
+            @pl.when(jnp.logical_not(here))
+            def _():
+                copy.start()
+
+            @pl.when(here)
+            def _():
+                brecv[r, slot] = bsend[p]
+
+    for part in range(1, x_parts):
+        for d in range(1, rows):
+            x_copy(d, part).start()
+    wo_copies = []
+    for d in range(1, heads):
+        copy = pltpu.make_async_remote_copy(
+            src_ref=wo, dst_ref=wobuf.at[d], send_sem=wo_send.at[d], recv_sem=wo_recv.at[d],
+            device_id={"head": lax.rem(h + d, heads)}, device_id_type=MESH,
+        )
+        copy.start()
+        wo_copies.append(copy)
+
     own_rows = wobuf.shape[1]
     share = wobuf.shape[2] // heads
 
@@ -187,13 +195,17 @@
     weight_out = pltpu.make_async_copy(owbuf, owout, local_sem.at[10])
     weight_out.start()
 
-    for d in range(1, rows):
-        x_copies[d - 1].wait()
-        source = lax.rem(r + rows - d, rows)
-        for first in range(0, n_i, step_i):
-            at = pl.ds(first * n_j, flat)
-            normed = layer_norm(xs[source, at, :].astype(F32)).astype(BF16)
-            kv[source, at, :] = dot_t(normed, wkv)
+    def take(part):
+        step_x = largest_divisor(part_i, 12, 2)
+        for d in range(1, rows):
+            x_copy(d, part).wait()
+            source = lax.rem(r + rows - d, rows)
+            for first in range(part * part_i, (part + 1) * part_i, step_x):
+                at = pl.ds(first * n_j, step_x * n_j)
+                normed = layer_norm(xs[source, at, :].astype(F32)).astype(BF16)
+                kv[source, at, :] = dot_t(normed, wkv)
+
+    take(0)
 
     slots = n_j // piece
     for slot in range(slots):
@@ -217,7 +229,7 @@
     )
 
     lanes_k = -(-n_k // 128) * 128
-    step_a = largest_divisor(n_i, max(2, 40 * 1024 // (n_h * n_j * lanes_k)), 2)
+    step_a = largest_divisor(n_i // 2, max(2, 40 * 1024 // (n_h * n_j * lanes_k)), 2)
     flat_a = step_a * n_j
     steps = n_i // step_a
 
@@ -271,13 +283,19 @@
         for d in range(1, heads):
             gated_copy(step, d, at).wait()
 
+    for part in range(x_parts):
+        if part > 0:
+            take(part)
+        low, high = part * part_i // step_a, (part + 1) * part_i // step_a
+        if steps <= 4:
+            for step in range(low, high):
+                attend(step)
+        else:
+            pl.loop(low, high)(attend)
     if steps <= 4:
-        for step in range(steps):
-            attend(step)
         for step in range(steps):
             finish(step)
     else:
-        pl.loop(0, steps)(attend)
         pl.loop(0, steps)(finish)
     weight_out.wait()
 
@@ -309,7 +327,7 @@
     total = n_i * n_j
     piece = min(n_i, n_j)
     lanes_k = -(-n_k // 128) * 128
-    step_a = largest_divisor(n_i, max(2, 40 * 1024 // (n_h * n_j * lanes_k)), 2)
+    step_a = largest_divisor(n_i // 2, max(2, 40 * 1024 // (n_h * n_j * lanes_k)), 2)
     steps = n_i // step_a
     share = w_out.shape[1] // heads
     hbm = pl.BlockSpec(memory_space=pltpu.HBM)
@@ -331,8 +349,8 @@
         pltpu.VMEM((total, 2 * hw), BF16),
         pltpu.VMEM((heads, 2 * hw, share), BF16),
         dma((11,)),
-        dma((rows,)),
-        dma((rows,)),
+        dma((rows, 2)),
+        dma((rows, 2)),
         dma((heads,)),
         dma((heads,)),
         dma((n_i // piece, cols)),

time: 13.5 us -> 13.5 us (level)
  no operation moved by 1% of the time
where the time goes in v3:
time: 13.5 us; the launch traced here: 13.3 us
  Pallas kernels  13.3 us (99%)
    pallas_call x1, Pallas kernels, per_device(): pl.pallas_call(functools.partial(kernel, (rows, cols, heads, n_i, n_j, n_...  11.6 us
    pallas_call x1, Pallas kernels, per_device(): pl.pallas_call(project, out_shape=jax.ShapeDtypeStruct((total, share), BF...  1.73 us

profile of v3, /device:TPU:0, one launch (start us, length us, event | category | flops | bytes accessed | tf_op | source)
XLA Modules:
  0.0 13.3 jit_solution(6632826870254661515)
XLA Ops:
  0.0 11.6 %shard_map.100 = (bf16[2,288,128]{2,1,0:T(8,128)(2,1)}, bf16[2,128,64]{2,1,0:T(8,128)(2,1)}) custom-call(bf16[288,128]{1,0:T(8,128)(2,1)} %bitcast.8, s32[1,48]{1,0:T(1,128)} %bitcast.13, s32[4]{0:T(128)} %breaks.1, f32[2]{0:T(128)} %chain_bias.1, bf16[64,128]{1,0:T(8,128)(2,1)} %bitcast.9, bf16[64,128]{1,0:T(8,128)(2,1)} %bitcast.10, ...), custom_call_target="tpu_custom_call" | custom-call | tf_op jit(solution)/shard_map/pallas_call | solution.py:362
  11.6 1.7 %shard_map.101 = bf16[288,64]{1,0:T(8,128)(2,1)} custom-call(bf16[2,288,128]{2,1,0:T(8,128)(2,1)} %get-tuple-element.7.gated, bf16[2,128,64]{2,1,0:T(8,128)(2,1)} %get-tuple-element.8.weights), custom_call_target="tpu_custom_call" | custom-call | tf_op jit(solution)/shard_map/pallas_call | solution.py:380
